TPU v7x, 32 devices: a whole 2x2x4 slice. The times are simulated.
32 devices in a mesh: parts: 2 (over x), blk: 16 (over z, y, core).
Axes of the slice: x: 2, y: 2, z: 4, core: 2. Of those that a mesh axis runs over, the one named last changes fastest.
Arguments:
- particles: bfloat16 [4096, 4608], P(('parts', 'blk')), parts along dimension 0, may hold values from -24 to 24
- references: bfloat16 [64, 4608], P(('parts', 'blk')), parts along dimension 0, may hold values from -0.5 to 0.5
- inv_noise: float32 [4096], P(('parts', 'blk')), parts along dimension 0, may hold values from 1 to 4
- assign: int32 [4096, 2], P(('parts', 'blk')), parts along dimension 0, may hold values from 0 to 31, all different within a row; in each aligned block of 128 rows (0 to 127, 128 to 255, ...) at most 16 rows name the same one
Outputs:
- class_sums: float32 [64, 4608], P(('parts', 'blk')), parts along dimension 0
- class_mass: float32 [64], P(('parts', 'blk')), parts along dimension 0
- log_evidence: float32 [4096], P(('parts', 'blk')), parts along dimension 0
There are 2 independent parts, one for each index of `parts`. A program takes and returns all parts, laid end to end along the dimension named above; each array names one. Nothing has to cross between parts.
Inputs may be any that keep to these rules, and one draw needn't show every extreme that they name: `assign`: among the rows of one device, at most 16 name any one class; in every draw some device's block reaches this bound.
All inputs are finite; a program needn't handle non-finite values.
Results may differ from a plain program's by a relative error of at most 0.0039.
Values may be sent and summed in bfloat16 or wider, within the bound.
A program may use at most 128 MiB of HBM per device.

v0:
```python
import jax
import jax.numpy as jnp
from jax import lax
from jax.sharding import PartitionSpec as P

ROT = 12
TOPK = 2
CYCLES = 12
ANGLES = 384


def local(particles, references, inv_noise, assign):
    local_rows = particles.shape[0]
    width = particles.shape[1]
    owned = references.shape[0]
    devices = lax.axis_size("blk")
    classes = owned * devices
    step = ANGLES // ROT
    piece = lax.all_gather(references, "blk", axis=0, tiled=True)
    count = piece.shape[0]
    cube = piece.reshape(count, CYCLES, ANGLES)
    turned = jnp.stack([jnp.roll(cube, r * step, axis=2) for r in range(ROT)], axis=1)
    turned = turned.reshape(count * ROT, width)
    dots = lax.dot_general(
        particles, turned, (((1,), (1,)), ((), ())), preferred_element_type=jnp.float32
    )
    energy = jnp.sum(jnp.square(piece.astype(jnp.float32)), axis=1)
    logits = inv_noise[:, None] * (dots - 0.5 * jnp.repeat(energy, ROT)[None, :])
    top = jnp.max(logits, axis=1, keepdims=True)
    total = jnp.sum(jnp.exp(logits - top), axis=1, keepdims=True)
    log_evidence = top + jnp.log(total)
    post = jnp.exp(logits - log_evidence).reshape(local_rows, classes, ROT)
    picked = jnp.take_along_axis(post, assign[:, :, None], axis=1)
    blocks_b = jnp.arange(ROT, dtype=jnp.int32)[:, None, None]
    blocks_c = jnp.arange(ROT, dtype=jnp.int32)[None, :, None]
    shifts = jnp.arange(ROT, dtype=jnp.int32)[None, None, :]
    circulant = ((blocks_c - blocks_b) % ROT == shifts).astype(jnp.float32)
    mixing = jnp.einsum("pjr,bcr->pjbc", picked, circulant, precision=lax.Precision.HIGHEST)
    blocked = particles.reshape(local_rows, CYCLES, ROT, step).transpose(0, 2, 1, 3)
    blocked = blocked.reshape(local_rows, ROT, CYCLES * step).astype(jnp.float32)
    summed = jnp.einsum("pjbc,pcm->pjbm", mixing, blocked, precision=lax.Precision.HIGHEST)
    summed = summed.astype(jnp.bfloat16).reshape(local_rows, TOPK, ROT, CYCLES, step)
    flat_rows = summed.transpose(0, 1, 3, 2, 4).reshape(local_rows * TOPK, width)
    flat_weights = jnp.sum(picked, axis=2).astype(jnp.bfloat16).reshape(local_rows * TOPK)
    flat_class = assign.reshape(local_rows * TOPK)
    selector = (flat_class[:, None] == jnp.arange(classes, dtype=jnp.int32)[None, :]).astype(
        jnp.bfloat16
    )
    partial_sums = lax.dot_general(
        selector, flat_rows, (((0,), (0,)), ((), ())), preferred_element_type=jnp.float32
    )
    partial_mass = lax.dot_general(
        selector,
        flat_weights[:, None],
        (((0,), (0,)), ((), ())),
        preferred_element_type=jnp.float32,
    )[:, 0]
    class_sums, class_mass = (
        lax.psum_scatter(partial_sums, "blk", scatter_dimension=0, tiled=True),
        lax.psum_scatter(partial_mass, "blk", scatter_dimension=0, tiled=True),
    )
    return (class_sums, class_mass, log_evidence[:, 0])


def solution(mesh):
    placed = (
        P(("parts", "blk"), None),
        P(("parts", "blk"), None),
        P(("parts", "blk")),
        P(("parts", "blk"), None),
    )
    return jax.shard_map(
        local,
        mesh=mesh,
        in_specs=placed,
        out_specs=(P(("parts", "blk"), None), P(("parts", "blk")), P(("parts", "blk"))),
        check_vma=False,
    )
```

profile of v0, /device:TPU:0, one launch (start us, length us, event | category | flops | bytes accessed | tf_op | source)
XLA Modules:
  0.0 207.3 jit_solution(18054935562386416470)
XLA Ops:
  7.2 24.1 %all-gather = bf16[16,2,4608]{2,1,0:T(2,128)(2,1)S(1)} all-gather(bf16[1,2,4608]{2,1,0:T(2,128)(2,1)} %bitcast.89), channel_id=1, replica_groups=mesh['parts'=2,'blk'=16] {'blk'}, dimensions={0}, use_global_device_ids=true | all-gather | bytes 313344 | tf_op jit(solution)/shard_map/all_gather | solution.py:19
  31.4 0.2 reshape.89
  31.6 0.2 fusion.27
  31.8 0.8 fusion.28
  32.5 0.2 stack.39
  32.7 0.2 fusion.29
  32.9 0.8 fusion.30
  33.7 0.2 fusion.31
  33.9 0.8 fusion.32
  34.7 0.8 fusion.33
  35.5 0.7 fusion.34
  36.2 0.9 fusion.35
  37.1 0.9 fusion.36
  38.0 0.9 fusion.37
  38.9 0.4 multiply_reduce_fusion
  39.3 0.5 compare_and_fusion
  39.8 0.7 copy.31
  40.6 1.2 fusion.1
  41.8 1.1 fusion.2
  42.9 1.1 fusion.3
  44.1 1.1 fusion.4
  45.1 1.2 fusion.5
  46.3 0.2 fusion.6
  46.7 1.1 fusion.8
  47.8 1.0 fusion.9
  48.8 1.0 fusion.10
  50.0 0.8 copy.32
  50.9 2.8 %copy.47 = bf16[48,8,12,384]{3,1,2,0:T(8,128)(2,1)} copy(bf16[48,8,12,384]{3,2,1,0:T(8,128)(2,1)S(1)} %bitcast.83) | data formatting | bytes 7077888
  54.0 1.0 copy.36
  55.0 3.1 %fusion.38 = (f32[128]{0:T(128)S(1)}, f32[384,128]{1,0:T(8,128)S(1)}) fusion(f32[384]{0:T(512)S(1)} %mul.27, bf16[384,4608]{1,0:T(8,128)(2,1)} %bitcast.87, bf16[128,4608]{1,0:T(8,128)(2,1)S(1)} %copy-done, f32[128]{0:T(128)S(1)} %copy-done.10), kind=kOutput, calls=%fused_computation.67 | convolution fusion | flops 453132160 | bytes 4917760 | tf_op jit(solution)/shard_map/dot_general | solution.py:24
  58.2 0.5 copy-done.9
  58.8 1.8 copy.34
  60.8 1.9 gather_fusion
  62.8 1.0 fusion.14
  63.8 2.9 %copy.38 = f32[128,2,12,12]{3,2,1,0:T(8,128)} copy(f32[128,2,12,12]{0,3,2,1:T(8,128)S(1)} %fusion.14) | data formatting | bytes 294912 | tf_op jit(solution)/shard_map/pjr,bcr->pjbc/dot_general | solution.py:38
  66.7 0.3 copy.37
  66.9 2.1 %copy.44 = bf16[128,12,384,1]{2,1,3,0:T(8,128)(2,1)} copy(bf16[128,12,384,1]{0,2,1,3:T(8,128)(2,1)S(1)} %bitcast.86) | data formatting | bytes 2359296 | tf_op jit(solution)/shard_map/reshape | solution.py:40
  69.0 4.6 %convolution_convert_fusion = bf16[128,2,12,384]{3,2,1,0:T(8,128)(2,1)S(1)} fusion(f32[128,2,12,12]{3,2,1,0:T(8,128)} %copy.38, bf16[128,12,384,1]{2,1,3,0:T(8,128)(2,1)} %copy.44), kind=kOutput, calls=%fused_computation.1 | convolution fusion | flops 171048960 | bytes 3686400 | tf_op jit(solution)/shard_map/pjbc,pcm->pjbm/dot_general | solution.py:41
  73.7 3.2 %copy.40 = bf16[128,2,12,384]{0,3,2,1:T(8,128)(2,1)} copy(bf16[128,2,12,384]{3,2,1,0:T(8,128)(2,1)S(1)} %convolution_convert_fusion) | data formatting | bytes 4718592 | tf_op jit(solution)/shard_map/convert_element_type | solution.py:42
  76.9 18.2 %copy.41 = bf16[128,2,12,12,32]{4,3,2,1,0:T(8,128)(2,1)} copy(bf16[128,2,12,12,32]{0,4,2,3,1:T(8,128)(2,1)} %bitcast.84) | data formatting | bytes 4718592 | tf_op jit(solution)/shard_map/transpose | solution.py:43
  95.1 13.2 %reshape.95 = bf16[256,4608]{1,0:T(8,128)(2,1)S(1)} reshape(bf16[128,2,12,12,32]{4,3,2,1,0:T(8,128)(2,1)} %copy.41) | data formatting | bytes 4718592 | tf_op jit(solution)/shard_map/reshape | solution.py:43
  108.4 1.4 fusion.12
  110.3 0.6 dynamic-slice
  111.5 0.2 convolution_bitcast_fusion
  111.7 30.0 %all-reduce.1 = f32[32]{0:T(128)S(1)} all-reduce(f32[32]{0:T(128)S(1)} %convolution_bitcast_fusion), channel_id=3, replica_groups=mesh['parts'=2,'blk'=16] {'blk'}, use_global_device_ids=true, to_apply=%region_5.6.clone | all-reduce | flops 32 | bytes 256
  141.7 0.6 dynamic-slice.3
  142.3 56.6 %all-reduce.4.cloned.1.call-done = f32[32,4608]{1,0:T(8,128)} async-done(((f32[32,4608]{1,0:T(8,128)}), f32[32,4608]{1,0:T(8,128)}) %all-reduce.4.cloned.1.call-update) | async-done | bytes 589840
  198.9 1.5 constant_dynamic-slice_fusion
  (45 shorter events, 1.7 us)
Async XLA Ops:
  7.2 191.7 %all-reduce.4.cloned.1.call-start = ((), (), s32[]{:S(2)}) async-start(), calls=%async_computation | async-start | bytes 1179648
  32.7 6.5 %copy-start.7 = (s32[128,2]{0,1:T(2,128)S(1)}, s32[128,2]{0,1:T(2,128)}, u32[]{:S(2)}) copy-start(s32[128,2]{0,1:T(2,128)} %param.7) | copy-start | bytes 3076
  38.9 7.7 %copy-start.1 = (bf16[32,12,224]{2,1,0:T(8,128)(2,1)S(1)}, bf16[32,12,224]{2,1,0:T(8,128)(2,1)}, u32[]{:S(2)}) copy-start(bf16[32,12,224]{2,1,0:T(8,128)(2,1)} %get-tuple-element.19) | copy-start | bytes 516100
  39.3 7.3 %copy-start.2 = (bf16[32,12,160]{2,1,0:T(8,128)(2,1)S(1)}, bf16[32,12,160]{2,1,0:T(8,128)(2,1)}, u32[]{:S(2)}) copy-start(bf16[32,12,160]{2,1,0:T(8,128)(2,1)} %get-tuple-element.21) | copy-start | bytes 368644
  40.5 5.8 %copy-start.3 = (bf16[32,12,192]{2,1,0:T(8,128)(2,1)S(1)}, bf16[32,12,192]{2,1,0:T(8,128)(2,1)}, u32[]{:S(2)}) copy-start(bf16[32,12,192]{2,1,0:T(8,128)(2,1)} %get-tuple-element.23) | copy-start | bytes 442372
  40.5 5.8 %copy-start.4 = (bf16[32,12,192]{2,1,0:T(8,128)(2,1)S(1)}, bf16[32,12,192]{2,1,0:T(8,128)(2,1)}, u32[]{:S(2)}) copy-start(bf16[32,12,192]{2,1,0:T(8,128)(2,1)} %get-tuple-element.24) | copy-start | bytes 442372
  40.5 9.3 %copy-start.5 = (bf16[32,12,32]{2,1,0:T(8,128)(2,1)S(1)}, bf16[32,12,32]{2,1,0:T(8,128)(2,1)}, u32[]{:S(2)}) copy-start(bf16[32,12,32]{2,1,0:T(8,128)(2,1)} %get-tuple-element.5) | copy-start | bytes 73732
  50.9 3.1 %copy-start = (bf16[128,4608]{1,0:T(8,128)(2,1)S(1)}, bf16[128,4608]{1,0:T(8,128)(2,1)}, u32[]{:S(2)}) copy-start(bf16[128,4608]{1,0:T(8,128)(2,1)} %param.4) | copy-start | bytes 3538948
  50.9 4.1 %copy-start.10 = (f32[128]{0:T(128)S(1)}, f32[128]{0:T(128)}, u32[]{:S(2)}) copy-start(f32[128]{0:T(128)} %param.6) | copy-start | bytes 1540
  58.2 0.5 copy-start.9
  95.1 13.2 %copy-start.6 = (s32[128,2]{1,0:T(8,128)S(1)}, s32[128,2]{1,0:T(8,128)}, u32[]{:S(2)}) copy-start(s32[128,2]{1,0:T(8,128)} %copy.31) | copy-start | bytes 3076
  95.1 14.9 %copy-start.8 = (pred[128,2]{0,1:T(4,128)(4,1)S(1)}, pred[128,2]{0,1:T(4,128)(4,1)}, u32[]{:S(2)}) copy-start(pred[128,2]{0,1:T(4,128)(4,1)} %compare_and_fusion) | copy-start | bytes 772
  95.1 15.2 %copy-start.11 = (u32[32]{0:T(128)S(1)}, u32[32]{0:T(128)}, u32[]{:S(2)}) copy-start(u32[32]{0:T(128)} %constant.47) | copy-start | bytes 388
Sparse Core Ops, SparseCore 0:
  110.0 88.8 all-reduce.3
where the time goes:
time: 208 us; the launch traced here: 207 us
  local copies, waits for them, and re-layouts  60.8 us (29%)
  waiting for transfers between devices  56.6 us (27%)
  blocking collectives  54.2 us (26%)
  between operations  14.9 us (7%)
  other arithmetic  10.5 us (5%)
  matrix products  10.3 us (5%)
    unnamed x2, waiting for transfers between devices  56.6 us
    unnamed x1, blocking collectives  30 us
    all_gather x1, blocking collectives, local(): piece = lax.all_gather(references, 'blk', axis=0, tiled=True)  24.1 us
    transpose x1, local copies, waits for them, and re-layouts, local(): summed.transpose(0, 1, 3, 2, 4).reshape(local_rows * TOPK, width)  18.2 us
    reshape x1, local copies, waits for them, and re-layouts, local(): summed.transpose(0, 1, 3, 2, 4).reshape(local_rows * TOPK, width)  13.2 us
    unnamed x10, other arithmetic  9.24 us
    unnamed x31, local copies, waits for them, and re-layouts  7.83 us
    slice x11, local copies, waits for them, and re-layouts, local(): jnp.roll(cube, r * step, axis=2)  7.09 us
  transfers between devices with their start and end apart: 1, of which 1 were waited for; matrix products, arithmetic and copies ran while one was open for 1% of the time, Pallas kernels for 0%

commit v1 on v0

v1 whole, which is shorter than its diff:
```python
import functools

import jax
import jax.numpy as jnp
from jax import lax
from jax.experimental import pallas as pl
from jax.experimental.pallas import tpu as pltpu
from jax.sharding import PartitionSpec as P

ROT = 12
TOPK = 2
CYCLES = 12
ANGLES = 384
STEP = ANGLES // ROT
LANES = 128
TURNS = ANGLES // LANES
SHIFTS = LANES // STEP
MESH = pl.DeviceIdType.MESH


def kernel(n, owned, block_rows, x_hbm, refs_ref, inv_ref, assign_ref, sums_ref, mass_ref, evid_ref,
           x_ref, held, work, part, landed, x_sem, send1, recv1, send2, recv2):
    me = lax.axis_index("blk")
    classes = n * owned
    rows = x_ref.shape[0]

    load = pltpu.make_async_copy(x_hbm, x_ref, x_sem)
    load.start()

    def ahead(d):
        return {"blk": lax.rem(me + d, n)}

    def behind(d):
        return {"blk": lax.rem(me + n - d, n)}

    barrier = pltpu.get_barrier_semaphore()
    for d in range(1, n):
        pl.semaphore_signal(barrier, inc=1, device_id=ahead(d), device_id_type=MESH)

    own = refs_ref[...].astype(jnp.float32)
    for b in range(TURNS):
        work[b, 0:block_rows, :] = jnp.zeros((block_rows, LANES), jnp.float32)
        for c in range(CYCLES):
            at = (c * TURNS + b) * LANES
            work[b, c * owned:(c + 1) * owned, :] = own[:, at:at + LANES]
        held[0, :, b * LANES:(b + 1) * LANES] = work[b, 0:block_rows, :].astype(jnp.bfloat16)

    pl.semaphore_wait(barrier, n - 1)

    gathers = []
    for d in range(1, n):
        copy = pltpu.make_async_remote_copy(
            src_ref=held.at[0], dst_ref=held.at[d], send_sem=send1.at[d], recv_sem=recv1.at[d],
            device_id=ahead(d), device_id_type=MESH)
        copy.start()
        gathers.append(copy)
    load.wait()
    for copy in gathers:
        copy.wait_recv()

    for d in range(n):
        for b in range(TURNS):
            work[b, d * block_rows:(d + 1) * block_rows, :] = held[d, :, b * LANES:(b + 1) * LANES].astype(jnp.float32)

    def shifted(c):
        blocks = [x_ref[:, (c * TURNS + b) * LANES:(c * TURNS + b + 1) * LANES] for b in range(TURNS)]
        return jnp.concatenate(
            [jnp.concatenate([blocks[(b + q) % TURNS] for b in range(TURNS)], axis=1)
             for q in range(TURNS)], axis=0)

    dots = jnp.zeros((SHIFTS * classes, TURNS * rows), jnp.float32)
    energy = jnp.zeros((classes, ANGLES), jnp.float32)
    for c in range(CYCLES):
        ref_c = jnp.concatenate(
            [jnp.concatenate([work[b, pl.ds(c * owned + k, n, stride=block_rows), :] for k in range(owned)], axis=0)
             for b in range(TURNS)], axis=1)
        energy += ref_c * ref_c
        turned = jnp.concatenate(
            [ref_c] + [pltpu.roll(ref_c, s * STEP, 1) for s in range(1, SHIFTS)], axis=0)
        dots += lax.dot_general(
            turned.astype(jnp.bfloat16), shifted(c), (((1,), (1,)), ((), ())),
            preferred_element_type=jnp.float32)

    half = 0.5 * jnp.sum(energy, axis=1, keepdims=True)
    half = jnp.concatenate([half] * SHIFTS, axis=0)
    inv = inv_ref[...]
    logits = jnp.concatenate([inv] * TURNS, axis=1) * (dots - half)

    def across(value, join):
        pieces = [value[:, q * rows:(q + 1) * rows] for q in range(TURNS)]
        return functools.reduce(join, pieces)

    top = across(jnp.max(logits, axis=0, keepdims=True), jnp.maximum)
    scaled = jnp.exp(logits - jnp.concatenate([top] * TURNS, axis=1))
    total = across(jnp.sum(scaled, axis=0, keepdims=True), jnp.add)
    evid_ref[...] = top + jnp.log(total)

    place = lax.broadcasted_iota(jnp.int32, (n, rows), 0)
    source = me - place
    source = jnp.where(source < 0, source + n, source) * owned
    names = jnp.concatenate([source + k for k in range(owned)], axis=0)
    named = names == assign_ref[0:1, :]
    for j in range(1, TOPK):
        named = jnp.logical_or(named, names == assign_ref[j:j + 1, :])
    picked = jnp.where(named, 1.0 / total, 0.0)
    picked = jnp.concatenate([picked] * TURNS, axis=1)
    weight = scaled * jnp.concatenate([picked] * SHIFTS, axis=0)
    mass = jnp.sum(weight, axis=1, keepdims=True)
    mass = functools.reduce(jnp.add, [mass[s * classes:(s + 1) * classes] for s in range(SHIFTS)])
    high = weight.astype(jnp.bfloat16)
    low = (weight - high.astype(jnp.float32)).astype(jnp.bfloat16)
    both = jnp.concatenate([high, low], axis=0)

    def put(row, value):
        for k in range(owned):
            for b in range(TURNS):
                work[b, pl.ds(row * owned + k, n, stride=block_rows), :] = value[k * n:(k + 1) * n, b * LANES:(b + 1) * LANES]

    for c in range(CYCLES):
        mixed = jnp.dot(both, shifted(c), preferred_element_type=jnp.float32)
        out = None
        for s in range(SHIFTS):
            piece = mixed[s * classes:(s + 1) * classes] + mixed[(SHIFTS + s) * classes:(SHIFTS + s + 1) * classes]
            if s:
                piece = pltpu.roll(piece, ANGLES - s * STEP, 1)
            out = piece if out is None else out + piece
        put(c, out)
    mass_high = mass.astype(jnp.bfloat16).astype(jnp.float32)
    lane = lax.broadcasted_iota(jnp.int32, (classes, ANGLES), 1)
    put(CYCLES, jnp.where(lane < LANES, mass_high, mass - mass_high))
    for d in range(n):
        for b in range(TURNS):
            part[d, :, b * LANES:(b + 1) * LANES] = work[b, d * block_rows:(d + 1) * block_rows, :].astype(jnp.bfloat16)

    scatters = []
    for d in range(1, n):
        copy = pltpu.make_async_remote_copy(
            src_ref=part.at[d], dst_ref=landed.at[d], send_sem=send2.at[d], recv_sem=recv2.at[d],
            device_id=behind(d), device_id_type=MESH)
        copy.start()
        scatters.append(copy)
    for copy in gathers:
        copy.wait_send()
    acc = jnp.concatenate([work[b, 0:block_rows, :] for b in range(TURNS)], axis=1)
    for d in range(1, n):
        scatters[d - 1].wait_recv()
        acc = acc + landed[d].astype(jnp.float32)
    for b in range(TURNS):
        work[b, 0:block_rows, :] = acc[:, b * LANES:(b + 1) * LANES]
    for c in range(CYCLES):
        for b in range(TURNS):
            at = (c * TURNS + b) * LANES
            sums_ref[:, at:at + LANES] = work[b, c * owned:(c + 1) * owned, :]
    tail = slice(CYCLES * owned, (CYCLES + 1) * owned)
    mass_ref[...] = work[0, tail, :] + work[1, tail, :]
    for copy in scatters:
        copy.wait_send()


def local(particles, references, inv_noise, assign):
    rows, width = particles.shape
    owned = references.shape[0]
    n = lax.axis_size("blk")
    block_rows = -(-owned * (CYCLES + 1) // 16) * 16
    vmem = pl.BlockSpec(memory_space=pltpu.VMEM)
    sums, mass, evid = pl.pallas_call(
        functools.partial(kernel, n, owned, block_rows),
        out_shape=(
            jax.ShapeDtypeStruct((owned, width), jnp.float32),
            jax.ShapeDtypeStruct((owned, LANES), jnp.float32),
            jax.ShapeDtypeStruct((1, rows), jnp.float32),
        ),
        in_specs=[pl.BlockSpec(memory_space=pl.ANY), vmem, vmem, vmem],
        out_specs=(vmem, vmem, vmem),
        scratch_shapes=[
            pltpu.VMEM((rows, width), jnp.bfloat16),
            pltpu.VMEM((n, block_rows, ANGLES), jnp.bfloat16),
            pltpu.VMEM((TURNS, n * block_rows, LANES), jnp.float32),
            pltpu.VMEM((n, block_rows, ANGLES), jnp.bfloat16),
            pltpu.VMEM((n, block_rows, ANGLES), jnp.bfloat16),
            pltpu.SemaphoreType.DMA,
            pltpu.SemaphoreType.DMA((n,)),
            pltpu.SemaphoreType.DMA((n,)),
            pltpu.SemaphoreType.DMA((n,)),
            pltpu.SemaphoreType.DMA((n,)),
        ],
        compiler_params=pltpu.CompilerParams(
            collective_id=0, has_side_effects=True, vmem_limit_bytes=48 * 1024 * 1024),
        cost_estimate=pl.CostEstimate(
            flops=6 * rows * n * owned * ROT * width, bytes_accessed=2 * rows * width, transcendentals=rows * n * owned * ROT),
    )(particles, references, inv_noise.reshape(1, rows), assign.T)
    return sums, mass[:, 0], evid.reshape(rows)


def solution(mesh):
    placed = (
        P(("parts", "blk"), None),
        P(("parts", "blk"), None),
        P(("parts", "blk")),
        P(("parts", "blk"), None),
    )
    return jax.shard_map(
        local,
        mesh=mesh,
        in_specs=placed,
        out_specs=(P(("parts", "blk"), None), P(("parts", "blk")), P(("parts", "blk"))),
        check_vma=False,
    )
```

time: 208 us -> 37.3 us (0.18)
  waiting for transfers between devices: 56.6 us -> 0 us
  local copies, waits for them, and re-layouts: 60.8 us -> 5.07 us
  blocking collectives: 54.2 us -> 0 us
  Pallas kernels: 0 us -> 31.3 us
  between operations: 14.9 us -> 0.65 us
  other arithmetic: 10.5 us -> 0 us
  matrix products: 10.3 us -> 0 us
    unnamed x2 -> x0, waiting for transfers between devices: 56.6 us -> none
    pallas_call x0 -> x1, Pallas kernels: none -> 31.3 us  [local(): pl.pallas_call(functools.partial(kernel, n, owned, block_rows), out_shape...]
    unnamed x1 -> x0, blocking collectives: 30 us -> none
    all_gather x1 -> x0, blocking collectives: 24.1 us -> none  [local(): piece = lax.all_gather(references, 'blk', axis=0, tiled=True)]
    transpose x2 -> x0, local copies, waits for them, and re-layouts: 18.5 us -> none  [the longest x1 18.2 us: local(): summed.transpose(0, 1, 3, 2, 4).reshape(local_rows * TOPK, width)]
    reshape x5 -> x0, local copies, waits for them, and re-layouts: 17.3 us -> none  [the longest x1 13.2 us: local(): summed.transpose(0, 1, 3, 2, 4).reshape(local_rows * TOPK, width)]
    dot_general x5 -> x0, matrix products: 10.3 us -> none  [the longest x1 4.62 us: local(): jnp.einsum('pjbc,pcm->pjbm', mixing, blocked, precision=lax.Precision.HIG...]
    unnamed x10 -> x0, other arithmetic: 9.24 us -> none
  transfers between devices with their start and end apart: 1 -> 0, of which waited for: 1 -> 0; matrix products, arithmetic and copies ran while one was open for 1% -> 0% of each run, Pallas kernels for 0% -> 0%
where the time goes in v1:
time: 37.3 us; the launch traced here: 37 us
  Pallas kernels  31.3 us (84%)
  local copies, waits for them, and re-layouts  5.07 us (14%)
  between operations  0.65 us (2%)
    pallas_call x1, Pallas kernels, local(): pl.pallas_call(functools.partial(kernel, n, owned, block_rows), out_shape...  31.3 us
    unnamed x10, local copies, waits for them, and re-layouts  4.45 us

profile of v1, /device:TPU:0, one launch (start us, length us, event | category | flops | bytes accessed | tf_op | source)
XLA Modules:
  0.0 37.0 jit_solution(7631364704176621310)
XLA Ops:
  0.6 0.0 copy-start
  0.6 1.3 %copy-done = bf16[128,4608]{1,0:T(8,128)(2,1)S(1)} copy-done((bf16[128,4608]{1,0:T(8,128)(2,1)S(1)}, bf16[128,4608]{1,0:T(8,128)(2,1)}, u32[]{:S(2)}) %copy-start) | copy-done | bytes 1179672
  1.9 0.0 copy-start.1
  1.9 0.7 %copy-done.1 = bf16[2,4608]{1,0:T(2,128)(2,1)S(1)} copy-done((bf16[2,4608]{1,0:T(2,128)(2,1)S(1)}, bf16[2,4608]{1,0:T(2,128)(2,1)}, u32[]{:S(2)}) %copy-start.1) | copy-done | bytes 18456
  2.6 0.0 copy-start.2
  2.6 0.7 %copy-done.2 = s32[128,2]{0,1:T(2,128)S(1)} copy-done((s32[128,2]{0,1:T(2,128)S(1)}, s32[128,2]{0,1:T(2,128)}, u32[]{:S(2)}) %copy-start.2) | copy-done | bytes 1048
  3.3 0.0 copy-start.3
  3.3 0.7 %copy-done.3 = f32[128]{0:T(128)S(1)} copy-done((f32[128]{0:T(128)S(1)}, f32[128]{0:T(128)}, u32[]{:S(2)}) %copy-start.3) | copy-done | bytes 536
  4.0 31.3 %shard_map.67 = (f32[2,4608]{1,0:T(2,128)S(1)}, f32[2,128]{1,0:T(2,128)S(1)}, f32[1,128]{1,0:T(1,128)S(1)}) custom-call(bf16[128,4608]{1,0:T(8,128)(2,1)S(1)} %copy-done, bf16[2,4608]{1,0:T(2,128)(2,1)S(1)} %copy-done.1, f32[1,128]{1,0:T(1,128)S(1)} %bitcast.4, s32[2,128]{1,0:T(2,128)S(1)} %bitcast.3), custom_call_target="tpu_custom_call" | custom-call | flops 1358954496 | bytes 1179648 | tf_op jit(solution)/shard_map/pallas_call | solution.py:166
  35.3 0.6 %slice_reduce_fusion = f32[2]{0:T(128)} fusion(f32[2,128]{1,0:T(2,128)S(1)} %get-tuple-element.7), kind=kLoop, calls=%fused_computation | loop fusion | bytes 16 | tf_op jit(solution)/shard_map/slice | solution.py:192
  35.9 0.6 %copy.9 = f32[2,4608]{1,0:T(2,128)} copy(f32[2,4608]{1,0:T(2,128)S(1)} %get-tuple-element.12) | data formatting | bytes 73728
  36.5 0.5 %copy.10 = f32[128]{0:T(128)} copy(f32[128]{0:T(128)S(1)} %bitcast.5) | data formatting | bytes 1024
Async XLA Ops:
  0.6 1.3 %copy-start = (bf16[128,4608]{1,0:T(8,128)(2,1)S(1)}, bf16[128,4608]{1,0:T(8,128)(2,1)}, u32[]{:S(2)}) copy-start(bf16[128,4608]{1,0:T(8,128)(2,1)} %x_hbm.1) | copy-start | bytes 3538948
  1.9 0.7 %copy-start.1 = (bf16[2,4608]{1,0:T(2,128)(2,1)S(1)}, bf16[2,4608]{1,0:T(2,128)(2,1)}, u32[]{:S(2)}) copy-start(bf16[2,4608]{1,0:T(2,128)(2,1)} %refs_ref.1) | copy-start | bytes 55300
  2.6 0.7 %copy-start.2 = (s32[128,2]{0,1:T(2,128)S(1)}, s32[128,2]{0,1:T(2,128)}, u32[]{:S(2)}) copy-start(s32[128,2]{0,1:T(2,128)} %param.7) | copy-start | bytes 3076
  3.3 0.7 %copy-start.3 = (f32[128]{0:T(128)S(1)}, f32[128]{0:T(128)}, u32[]{:S(2)}) copy-start(f32[128]{0:T(128)} %param.6) | copy-start | bytes 1540

commit v2 on v1

v2 whole, which is shorter than its diff:
```python
import functools

import jax
import jax.numpy as jnp
from jax import lax
from jax.experimental import pallas as pl
from jax.experimental.pallas import tpu as pltpu
from jax.sharding import PartitionSpec as P

ROT = 12
TOPK = 2
CYCLES = 12
ANGLES = 384
STEP = ANGLES // ROT
LANES = 128
TURNS = ANGLES // LANES
SHIFTS = LANES // STEP
DEPTH = 16
MESH = pl.DeviceIdType.MESH


def kernel(n, owned, parts_in, parts_out, x_hbm, refs_hbm, inv_hbm, assign_hbm, sums_ref, mass_ref, evid_ref,
           x_ref, refs_ref, inv_ref, assign_ref, work, *scratch):
    lots = len(parts_in), len(parts_out)
    held, scratch = scratch[:lots[0]], scratch[lots[0]:]
    swap, scratch = scratch[:lots[1]], scratch[lots[1]:]
    swapped, scratch = scratch[:lots[1]], scratch[lots[1]:]
    part, scratch = scratch[:lots[1]], scratch[lots[1]:]
    landed, scratch = scratch[:lots[1]], scratch[lots[1]:]
    x_sem, small_sem, send1, recv1, swap_send, swap_recv, send2, recv2 = scratch
    me = lax.axis_index("blk")
    chips = n // 2
    chip, core = me // 2, lax.rem(me, 2)
    classes = n * owned
    rows = x_ref.shape[0]
    other = {"blk": chip * 2 + 1 - core}

    def ahead(d):
        return {"blk": lax.rem(chip + d, chips) * 2 + core}

    def behind(d):
        return {"blk": lax.rem(chip + chips - d, chips) * 2 + core}

    loads = [pltpu.make_async_copy(src, dst, small_sem.at[i]) for i, (src, dst) in enumerate(
        ((refs_hbm, refs_ref), (inv_hbm, inv_ref), (assign_hbm, assign_ref)))]
    loads.append(pltpu.make_async_copy(x_hbm, x_ref, x_sem))
    for load in loads:
        load.start()

    barrier = pltpu.get_barrier_semaphore()
    pl.semaphore_signal(barrier, inc=1, device_id=other, device_id_type=MESH)
    for d in range(1, chips):
        pl.semaphore_signal(barrier, inc=1, device_id=ahead(d), device_id_type=MESH)

    def spot(c, b, k):
        at = (c * TURNS + b) * owned + k
        return at // DEPTH, at % DEPTH

    loads[0].wait()
    own = refs_ref[...].astype(jnp.float32)
    for j in range(work.shape[0]):
        work[j, 0:DEPTH, :] = jnp.zeros((DEPTH, LANES), jnp.float32)
    for c in range(CYCLES):
        for b in range(TURNS):
            at = (c * TURNS + b) * LANES
            for k in range(owned):
                j, row = spot(c, b, k)
                work[j, row:row + 1, :] = own[k:k + 1, at:at + LANES]

    def each(parts):
        first = 0
        for lot, count in enumerate(parts):
            yield lot, first, count
            first += count

    for lot, first, count in each(parts_in):
        for j in range(count):
            held[lot][0, :, j * LANES:(j + 1) * LANES] = work[first + j, 0:DEPTH, :].astype(jnp.bfloat16)

    pl.semaphore_wait(barrier, chips)

    def move(lot, src, dst, to):
        copy = pltpu.make_async_remote_copy(
            src_ref=held[lot].at[src], dst_ref=held[lot].at[dst], send_sem=send1.at[lot, dst],
            recv_sem=recv1.at[lot, dst], device_id=to, device_id_type=MESH)
        copy.start()
        return copy

    gathers = []
    for lot, _, _ in each(parts_in):
        copies = {d: move(lot, 0, d, ahead(d)) for d in range(1, chips)}
        copies[chips] = move(lot, 0, chips, other)
        gathers.append(copies)
    for load in loads[1:]:
        load.wait()

    def shifted(c):
        blocks = [x_ref[:, (c * TURNS + b) * LANES:(c * TURNS + b + 1) * LANES] for b in range(TURNS)]
        return jnp.concatenate(
            [jnp.concatenate([blocks[(b + q) % TURNS] for b in range(TURNS)], axis=1)
             for q in range(TURNS)], axis=0)

    def spread(lot, first, count):
        copies = gathers[lot]
        for d in range(1, chips):
            copies[d].wait_recv()
            copies[chips + d] = move(lot, d, chips + d, other)
        for d in range(chips):
            copies[chips + d].wait_recv()
        for d in range(n):
            for j in range(count):
                work[first + j, d * DEPTH:(d + 1) * DEPTH, :] = (
                    held[lot][d, :, j * LANES:(j + 1) * LANES].astype(jnp.float32))

    dots = jnp.zeros((SHIFTS * classes, TURNS * rows), jnp.float32)
    energy = jnp.zeros((classes, ANGLES), jnp.float32)
    lots_left = list(each(parts_in))
    ready = 0
    for c in range(CYCLES):
        while ready <= spot(c, TURNS - 1, owned - 1)[0]:
            lot, first, count = lots_left.pop(0)
            spread(lot, first, count)
            ready = first + count
        pieces = []
        for b in range(TURNS):
            column = []
            for k in range(owned):
                j, row = spot(c, b, k)
                column.append(work[j, pl.ds(row, n, stride=DEPTH), :])
            pieces.append(jnp.concatenate(column, axis=0))
        ref_c = jnp.concatenate(pieces, axis=1)
        energy += ref_c * ref_c
        turned = jnp.concatenate(
            [ref_c] + [pltpu.roll(ref_c, s * STEP, 1) for s in range(1, SHIFTS)], axis=0)
        dots += lax.dot_general(
            turned.astype(jnp.bfloat16), shifted(c), (((1,), (1,)), ((), ())),
            preferred_element_type=jnp.float32)

    half = 0.5 * jnp.sum(energy, axis=1, keepdims=True)
    half = jnp.concatenate([half] * SHIFTS, axis=0)
    inv = inv_ref[...]
    logits = jnp.concatenate([inv] * TURNS, axis=1) * (dots - half)

    def across(value, join):
        return functools.reduce(join, [value[:, q * rows:(q + 1) * rows] for q in range(TURNS)])

    top = across(jnp.max(logits, axis=0, keepdims=True), jnp.maximum)
    scaled = jnp.exp(logits - jnp.concatenate([top] * TURNS, axis=1))
    total = across(jnp.sum(scaled, axis=0, keepdims=True), jnp.add)
    evid_ref[...] = top + jnp.log(total)

    slot = lax.broadcasted_iota(jnp.int32, (n, rows), 0)
    side = (slot >= chips).astype(jnp.int32)
    source = chip - (slot - side * chips)
    source = jnp.where(source < 0, source + chips, source) * 2 + jnp.where(side == 0, core, 1 - core)
    names = jnp.concatenate([source * owned + k for k in range(owned)], axis=0)
    named = names == assign_ref[0:1, :]
    for j in range(1, TOPK):
        named = jnp.logical_or(named, names == assign_ref[j:j + 1, :])
    picked = jnp.where(named, 1.0 / total, 0.0)
    picked = jnp.concatenate([picked] * TURNS, axis=1)
    weight = scaled * jnp.concatenate([picked] * SHIFTS, axis=0)
    high = weight.astype(jnp.bfloat16)
    low = (weight - high.astype(jnp.float32)).astype(jnp.bfloat16)
    both = jnp.concatenate([high, low], axis=0)
    mass = jnp.sum(weight, axis=1, keepdims=True)
    mass = functools.reduce(jnp.add, [mass[s * classes:(s + 1) * classes] for s in range(SHIFTS)])

    def put(c, b, value):
        for k in range(owned):
            j, row = spot(c, b, k)
            work[j, pl.ds(row, n, stride=DEPTH), :] = value[k * n:(k + 1) * n]

    mass = jnp.broadcast_to(mass, (classes, LANES))
    mass_high = mass.astype(jnp.bfloat16).astype(jnp.float32)
    lane = lax.broadcasted_iota(jnp.int32, (classes, LANES), 1)
    put(CYCLES, 0, jnp.where(lane < LANES // 2, mass_high, mass - mass_high))

    swaps, scatters = [], []

    def give(lot, first, count):
        for d in range(chips):
            for j in range(count):
                swap[lot][d, :, j * LANES:(j + 1) * LANES] = (
                    work[first + j, (chips + d) * DEPTH:(chips + d + 1) * DEPTH, :].astype(jnp.bfloat16))
        copy = pltpu.make_async_remote_copy(
            src_ref=swap[lot], dst_ref=swapped[lot], send_sem=swap_send.at[lot], recv_sem=swap_recv.at[lot],
            device_id=other, device_id_type=MESH)
        copy.start()
        swaps.append(copy)

    def pass_on(lot, first, count):
        swaps[lot].wait_recv()
        for d in (*range(1, chips), 0):
            for j in range(count):
                both_cores = (work[first + j, d * DEPTH:(d + 1) * DEPTH, :]
                              + swapped[lot][d, :, j * LANES:(j + 1) * LANES].astype(jnp.float32))
                if d:
                    part[lot][d, :, j * LANES:(j + 1) * LANES] = both_cores.astype(jnp.bfloat16)
                else:
                    work[first + j, 0:DEPTH, :] = both_cores
            if d:
                copy = pltpu.make_async_remote_copy(
                    src_ref=part[lot].at[d], dst_ref=landed[lot].at[d], send_sem=send2.at[lot, d],
                    recv_sem=recv2.at[lot, d], device_id=behind(d), device_id_type=MESH)
                copy.start()
                scatters.append((lot, d, first, count, copy))

    lots_left = list(each(parts_out))
    given = []
    for c in range(CYCLES):
        mixed = jnp.dot(both, shifted(c), preferred_element_type=jnp.float32)
        out = None
        for s in range(SHIFTS):
            piece = mixed[s * classes:(s + 1) * classes] + mixed[(SHIFTS + s) * classes:(SHIFTS + s + 1) * classes]
            if s:
                piece = pltpu.roll(piece, ANGLES - s * STEP, 1)
            out = piece if out is None else out + piece
        for b in range(TURNS):
            put(c, b, out[:, b * LANES:(b + 1) * LANES])
        if given and given[0][0] + 3 <= c:
            pass_on(*given.pop(0)[1])
        done = (c + 1) * TURNS * owned
        while lots_left and (done >= (lots_left[0][1] + lots_left[0][2]) * DEPTH or c == CYCLES - 1):
            give(*lots_left[0])
            given.append((c, lots_left.pop(0)))
    for _, lot in given:
        pass_on(*lot)

    for copies in gathers:
        for copy in copies.values():
            copy.wait_send()
    for copy in swaps:
        copy.wait_send()
    for lot, first, count in each(parts_out):
        mine = [one for one in scatters if one[0] == lot]
        acc = [work[first + j, 0:DEPTH, :] for j in range(count)]
        for _, d, _, _, copy in mine:
            copy.wait_recv()
            for j in range(count):
                acc[j] = acc[j] + landed[lot][d, :, j * LANES:(j + 1) * LANES].astype(jnp.float32)
        for j in range(count):
            work[first + j, 0:DEPTH, :] = acc[j]
    for c in range(CYCLES):
        for b in range(TURNS):
            at = (c * TURNS + b) * LANES
            for k in range(owned):
                j, row = spot(c, b, k)
                sums_ref[k:k + 1, at:at + LANES] = work[j, row:row + 1, :]
    for k in range(owned):
        j, row = spot(CYCLES, 0, k)
        tail = work[j, row:row + 1, :]
        mass_ref[k:k + 1, :] = tail + pltpu.roll(tail, LANES // 2, 1)
    for *_, copy in scatters:
        copy.wait_send()


def local(particles, references, inv_noise, assign):
    rows, width = particles.shape
    owned = references.shape[0]
    n = lax.axis_size("blk")
    chips = n // 2
    columns = -(-(CYCLES * TURNS + 1) * owned // DEPTH)
    parts_in = (columns - columns * 2 // 5, columns * 2 // 5)
    parts_out = parts_in[::-1]
    vmem = pl.BlockSpec(memory_space=pltpu.VMEM)
    hbm = pl.BlockSpec(memory_space=pltpu.HBM)

    def slots(count, parts):
        return [pltpu.VMEM((count, DEPTH, part * LANES), jnp.bfloat16) for part in parts]

    sums, mass, evid = pl.pallas_call(
        functools.partial(kernel, n, owned, parts_in, parts_out),
        out_shape=(
            jax.ShapeDtypeStruct((owned, width), jnp.float32),
            jax.ShapeDtypeStruct((owned, LANES), jnp.float32),
            jax.ShapeDtypeStruct((1, rows), jnp.float32),
        ),
        in_specs=[hbm] * 4,
        out_specs=(vmem, vmem, vmem),
        scratch_shapes=[
            pltpu.VMEM((rows, width), jnp.bfloat16),
            pltpu.VMEM((owned, width), jnp.bfloat16),
            pltpu.VMEM((1, rows), jnp.float32),
            pltpu.VMEM((TOPK, rows), jnp.int32),
            pltpu.VMEM((columns, n * DEPTH, LANES), jnp.float32),
            *slots(n, parts_in),
            *slots(chips, parts_out),
            *slots(chips, parts_out),
            *slots(chips, parts_out),
            *slots(chips, parts_out),
            pltpu.SemaphoreType.DMA,
            pltpu.SemaphoreType.DMA((3,)),
            pltpu.SemaphoreType.DMA((2, n)),
            pltpu.SemaphoreType.DMA((2, n)),
            pltpu.SemaphoreType.DMA((2,)),
            pltpu.SemaphoreType.DMA((2,)),
            pltpu.SemaphoreType.DMA((2, chips)),
            pltpu.SemaphoreType.DMA((2, chips)),
        ],
        compiler_params=pltpu.CompilerParams(
            collective_id=0, has_side_effects=True, vmem_limit_bytes=48 * 1024 * 1024),
        cost_estimate=pl.CostEstimate(
            flops=6 * rows * n * owned * ROT * width, bytes_accessed=2 * rows * width, transcendentals=rows * n * owned * ROT),
    )(particles, references, inv_noise.reshape(1, rows), assign.T)
    return sums, mass[:, 0], evid.reshape(rows)


def solution(mesh):
    placed = (
        P(("parts", "blk"), None),
        P(("parts", "blk"), None),
        P(("parts", "blk")),
        P(("parts", "blk"), None),
    )
    return jax.shard_map(
        local,
        mesh=mesh,
        in_specs=placed,
        out_specs=(P(("parts", "blk"), None), P(("parts", "blk")), P(("parts", "blk"))),
        check_vma=False,
    )
```

time: 37.3 us -> 30.4 us (0.82)
  Pallas kernels: 31.3 us -> 24.4 us
    pallas_call x1, Pallas kernels: 31.3 us -> 24.4 us  [local(): pl.pallas_call(functools.partial(kernel, n, owned, parts_in, parts_out),...]
where the time goes in v2:
time: 30.4 us; the launch traced here: 30.1 us
  Pallas kernels  24.4 us (80%)
  local copies, waits for them, and re-layouts  5.07 us (17%)
  between operations  0.65 us (2%)
    pallas_call x1, Pallas kernels, local(): pl.pallas_call(functools.partial(kernel, n, owned, parts_in, parts_out),...  24.4 us
    unnamed x10, local copies, waits for them, and re-layouts  4.45 us
    slice x1, local copies, waits for them, and re-layouts, local(): return (sums, mass[:, 0], evid.reshape(rows))  0.63 us

profile of v2, /device:TPU:0, one launch (start us, length us, event | category | flops | bytes accessed | tf_op | source)
XLA Modules:
  0.0 30.1 jit_solution(15255148499544716019)
XLA Ops:
  0.6 0.0 copy-start
  0.6 1.3 %copy-done = bf16[128,4608]{1,0:T(8,128)(2,1)S(1)} copy-done((bf16[128,4608]{1,0:T(8,128)(2,1)S(1)}, bf16[128,4608]{1,0:T(8,128)(2,1)}, u32[]{:S(2)}) %copy-start) | copy-done | bytes 1179672
  1.9 0.0 copy-start.1
  1.9 0.7 %copy-done.1 = bf16[2,4608]{1,0:T(2,128)(2,1)S(1)} copy-done((bf16[2,4608]{1,0:T(2,128)(2,1)S(1)}, bf16[2,4608]{1,0:T(2,128)(2,1)}, u32[]{:S(2)}) %copy-start.1) | copy-done | bytes 18456
  2.6 0.0 copy-start.2
  2.6 0.7 %copy-done.2 = s32[128,2]{0,1:T(2,128)S(1)} copy-done((s32[128,2]{0,1:T(2,128)S(1)}, s32[128,2]{0,1:T(2,128)}, u32[]{:S(2)}) %copy-start.2) | copy-done | bytes 1048
  3.3 0.0 copy-start.3
  3.3 0.7 %copy-done.3 = f32[128]{0:T(128)S(1)} copy-done((f32[128]{0:T(128)S(1)}, f32[128]{0:T(128)}, u32[]{:S(2)}) %copy-start.3) | copy-done | bytes 536
  4.0 24.4 %shard_map.67 = (f32[2,4608]{1,0:T(2,128)S(1)}, f32[2,128]{1,0:T(2,128)S(1)}, f32[1,128]{1,0:T(1,128)S(1)}) custom-call(bf16[128,4608]{1,0:T(8,128)(2,1)S(1)} %copy-done, bf16[2,4608]{1,0:T(2,128)(2,1)S(1)} %copy-done.1, f32[1,128]{1,0:T(1,128)S(1)} %bitcast.4, s32[2,128]{1,0:T(2,128)S(1)} %bitcast.3), custom_call_target="tpu_custom_call" | custom-call | flops 1358954496 | bytes 1179648 | tf_op jit(solution)/shard_map/pallas_call | solution.py:272
  28.4 0.6 %slice_reduce_fusion = f32[2]{0:T(128)} fusion(f32[2,128]{1,0:T(2,128)S(1)} %get-tuple-element.7), kind=kLoop, calls=%fused_computation | loop fusion | bytes 16 | tf_op jit(solution)/shard_map/slice | solution.py:306
  29.0 0.6 %copy.9 = f32[2,4608]{1,0:T(2,128)} copy(f32[2,4608]{1,0:T(2,128)S(1)} %get-tuple-element.12) | data formatting | bytes 73728
  29.6 0.5 %copy.10 = f32[128]{0:T(128)} copy(f32[128]{0:T(128)S(1)} %bitcast.5) | data formatting | bytes 1024
Async XLA Ops:
  0.6 1.3 %copy-start = (bf16[128,4608]{1,0:T(8,128)(2,1)S(1)}, bf16[128,4608]{1,0:T(8,128)(2,1)}, u32[]{:S(2)}) copy-start(bf16[128,4608]{1,0:T(8,128)(2,1)} %x_hbm.1) | copy-start | bytes 3538948
  1.9 0.7 %copy-start.1 = (bf16[2,4608]{1,0:T(2,128)(2,1)S(1)}, bf16[2,4608]{1,0:T(2,128)(2,1)}, u32[]{:S(2)}) copy-start(bf16[2,4608]{1,0:T(2,128)(2,1)} %refs_hbm.1) | copy-start | bytes 55300
  2.6 0.7 %copy-start.2 = (s32[128,2]{0,1:T(2,128)S(1)}, s32[128,2]{0,1:T(2,128)}, u32[]{:S(2)}) copy-start(s32[128,2]{0,1:T(2,128)} %param.7) | copy-start | bytes 3076
  3.3 0.7 %copy-start.3 = (f32[128]{0:T(128)S(1)}, f32[128]{0:T(128)}, u32[]{:S(2)}) copy-start(f32[128]{0:T(128)} %param.6) | copy-start | bytes 1540

commit v3 on v2

--- a/solution.py
+++ b/solution.py
@@ -20,7 +20,7 @@
 
 
 def kernel(n, owned, parts_in, parts_out, x_hbm, refs_hbm, inv_hbm, assign_hbm, sums_ref, mass_ref, evid_ref,
-           x_ref, refs_ref, inv_ref, assign_ref, work, *scratch):
+           x_ref, xt_ref, refs_ref, inv_ref, assign_ref, work, *scratch):
     lots = len(parts_in), len(parts_out)
     held, scratch = scratch[:lots[0]], scratch[lots[0]:]
     swap, scratch = scratch[:lots[1]], scratch[lots[1]:]
@@ -93,6 +93,8 @@
         gathers.append(copies)
     for load in loads[1:]:
         load.wait()
+    for at in range(0, x_ref.shape[1], LANES):
+        xt_ref[at:at + LANES, :] = x_ref[:, at:at + LANES].T
 
     def shifted(c):
         blocks = [x_ref[:, (c * TURNS + b) * LANES:(c * TURNS + b + 1) * LANES] for b in range(TURNS)]
@@ -112,8 +114,9 @@
                 work[first + j, d * DEPTH:(d + 1) * DEPTH, :] = (
                     held[lot][d, :, j * LANES:(j + 1) * LANES].astype(jnp.float32))
 
-    dots = jnp.zeros((SHIFTS * classes, TURNS * rows), jnp.float32)
+    dots = jnp.zeros((ROT * classes, rows), jnp.float32)
     energy = jnp.zeros((classes, ANGLES), jnp.float32)
+    turned = []
     lots_left = list(each(parts_in))
     ready = 0
     for c in range(CYCLES):
@@ -130,23 +133,23 @@
             pieces.append(jnp.concatenate(column, axis=0))
         ref_c = jnp.concatenate(pieces, axis=1)
         energy += ref_c * ref_c
-        turned = jnp.concatenate(
-            [ref_c] + [pltpu.roll(ref_c, s * STEP, 1) for s in range(1, SHIFTS)], axis=0)
-        dots += lax.dot_general(
-            turned.astype(jnp.bfloat16), shifted(c), (((1,), (1,)), ((), ())),
-            preferred_element_type=jnp.float32)
+        shifts = jnp.concatenate(
+            [ref_c] + [pltpu.roll(ref_c, s * STEP, 1) for s in range(1, SHIFTS)], axis=0).astype(jnp.bfloat16)
+        blocks = [shifts[:, b * LANES:(b + 1) * LANES] for b in range(TURNS)]
+        turned.append(jnp.concatenate(
+            [jnp.concatenate([blocks[(b - q) % TURNS] for b in range(TURNS)], axis=1)
+             for q in range(TURNS)], axis=0))
+        if len(turned) == 2:
+            dots += jnp.dot(
+                jnp.concatenate(turned, axis=1), xt_ref[(c - 1) * ANGLES:(c + 1) * ANGLES, :],
+                preferred_element_type=jnp.float32)
+            turned = []
 
     half = 0.5 * jnp.sum(energy, axis=1, keepdims=True)
-    half = jnp.concatenate([half] * SHIFTS, axis=0)
-    inv = inv_ref[...]
-    logits = jnp.concatenate([inv] * TURNS, axis=1) * (dots - half)
-
-    def across(value, join):
-        return functools.reduce(join, [value[:, q * rows:(q + 1) * rows] for q in range(TURNS)])
-
-    top = across(jnp.max(logits, axis=0, keepdims=True), jnp.maximum)
-    scaled = jnp.exp(logits - jnp.concatenate([top] * TURNS, axis=1))
-    total = across(jnp.sum(scaled, axis=0, keepdims=True), jnp.add)
+    logits = inv_ref[...] * (dots - jnp.concatenate([half] * ROT, axis=0))
+    top = jnp.max(logits, axis=0, keepdims=True)
+    scaled = jnp.exp(logits - top)
+    total = jnp.sum(scaled, axis=0, keepdims=True)
     evid_ref[...] = top + jnp.log(total)
 
     slot = lax.broadcasted_iota(jnp.int32, (n, rows), 0)
@@ -158,13 +161,14 @@
     for j in range(1, TOPK):
         named = jnp.logical_or(named, names == assign_ref[j:j + 1, :])
     picked = jnp.where(named, 1.0 / total, 0.0)
-    picked = jnp.concatenate([picked] * TURNS, axis=1)
-    weight = scaled * jnp.concatenate([picked] * SHIFTS, axis=0)
+    weight = scaled * jnp.concatenate([picked] * ROT, axis=0)
+    mass = functools.reduce(jnp.add, [weight[r * classes:(r + 1) * classes] for r in range(ROT)])
+    mass = jnp.sum(mass, axis=1, keepdims=True)
+    turn = SHIFTS * classes
+    weight = jnp.concatenate([weight[q * turn:(q + 1) * turn] for q in range(TURNS)], axis=1)
     high = weight.astype(jnp.bfloat16)
     low = (weight - high.astype(jnp.float32)).astype(jnp.bfloat16)
     both = jnp.concatenate([high, low], axis=0)
-    mass = jnp.sum(weight, axis=1, keepdims=True)
-    mass = functools.reduce(jnp.add, [mass[s * classes:(s + 1) * classes] for s in range(SHIFTS)])
 
     def put(c, b, value):
         for k in range(owned):
@@ -280,6 +284,7 @@
         out_specs=(vmem, vmem, vmem),
         scratch_shapes=[
             pltpu.VMEM((rows, width), jnp.bfloat16),
+            pltpu.VMEM((width, rows), jnp.bfloat16),
             pltpu.VMEM((owned, width), jnp.bfloat16),
             pltpu.VMEM((1, rows), jnp.float32),
             pltpu.VMEM((TOPK, rows), jnp.int32),
@@ -299,7 +304,7 @@
             pltpu.SemaphoreType.DMA((2, chips)),
         ],
         compiler_params=pltpu.CompilerParams(
-            collective_id=0, has_side_effects=True, vmem_limit_bytes=48 * 1024 * 1024),
+            collective_id=0, has_side_effects=True, vmem_limit_bytes=64 * 1024 * 1024 - 65536),
         cost_estimate=pl.CostEstimate(
             flops=6 * rows * n * owned * ROT * width, bytes_accessed=2 * rows * width, transcendentals=rows * n * owned * ROT),
     )(particles, references, inv_noise.reshape(1, rows), assign.T)

time: 30.4 us -> 30.7 us (level)
  Pallas kernels: 24.4 us -> 26 us
  local copies, waits for them, and re-layouts: 5.07 us -> 3.82 us
    unnamed x10 -> x2, local copies, waits for them, and re-layouts: 4.45 us -> 2.53 us
    pallas_call x1, Pallas kernels: 24.4 us -> 26 us  [local(): pl.pallas_call(functools.partial(kernel, n, owned, parts_in, parts_out),...]
    slice x1, local copies, waits for them, and re-layouts: 0.63 us -> 1.29 us  [local(): return (sums, mass[:, 0], evid.reshape(rows))]
where the time goes in v3:
time: 30.7 us; the launch traced here: 30.5 us
  Pallas kernels  26 us (85%)
  local copies, waits for them, and re-layouts  3.82 us (12%)
  between operations  0.64 us (2%)
    pallas_call x1, Pallas kernels, local(): pl.pallas_call(functools.partial(kernel, n, owned, parts_in, parts_out),...  26 us
    unnamed x2, local copies, waits for them, and re-layouts  2.53 us
    slice x1, local copies, waits for them, and re-layouts, local(): return (sums, mass[:, 0], evid.reshape(rows))  1.29 us

profile of v3, /device:TPU:0, one launch (start us, length us, event | category | flops | bytes accessed | tf_op | source)
XLA Modules:
  0.0 30.5 jit_solution(1796523765954966726)
XLA Ops:
  0.6 26.0 %shard_map.67 = (f32[2,4608]{1,0:T(2,128)}, f32[2,128]{1,0:T(2,128)}, f32[1,128]{1,0:T(1,128)}) custom-call(bf16[128,4608]{1,0:T(8,128)(2,1)} %x_hbm.1, bf16[2,4608]{1,0:T(2,128)(2,1)} %refs_hbm.1, f32[1,128]{1,0:T(1,128)} %bitcast.4, s32[2,128]{1,0:T(2,128)} %bitcast.3), custom_call_target="tpu_custom_call" | custom-call | flops 1358954496 | bytes 1179648 | tf_op jit(solution)/shard_map/pallas_call | solution.py:276
  26.7 1.3 %slice_reduce_fusion = f32[2]{0:T(128)} fusion(f32[2,128]{1,0:T(2,128)} %get-tuple-element.7), kind=kLoop, calls=%fused_computation | loop fusion | bytes 16 | tf_op jit(solution)/shard_map/slice | solution.py:311
  27.9 1.4 %copy.9 = f32[2,4608]{1,0:T(2,128)} copy(f32[2,4608]{1,0:T(2,128)} %get-tuple-element.12) | data formatting | bytes 73728
  29.3 1.1 %copy.10 = f32[128]{0:T(128)} copy(f32[128]{0:T(128)} %bitcast.5) | data formatting | bytes 1024

commit v4 on v3

--- a/solution.py
+++ b/solution.py
@@ -19,15 +19,28 @@
 MESH = pl.DeviceIdType.MESH
 
 
-def kernel(n, owned, parts_in, parts_out, x_hbm, refs_hbm, inv_hbm, assign_hbm, sums_ref, mass_ref, evid_ref,
-           x_ref, xt_ref, refs_ref, inv_ref, assign_ref, work, *scratch):
+def spot(owned, c, b, k):
+    at = (c * TURNS + b) * owned + k
+    return at // DEPTH, at % DEPTH
+
+
+def each(parts):
+    first = 0
+    for lot, count in enumerate(parts):
+        yield lot, first, count
+        first += count
+
+
+def kernel(n, owned, parts_in, parts_out, x_hbm, refs_hbm, inv_hbm, assign_hbm, *scratch):
     lots = len(parts_in), len(parts_out)
+    landed, scratch = scratch[:lots[1]], scratch[lots[1]:]
+    own_hbm, evid_hbm, x_ref, xt_ref, refs_ref, inv_ref, assign_ref, evid_ref, work = scratch[:9]
+    scratch = scratch[9:]
     held, scratch = scratch[:lots[0]], scratch[lots[0]:]
     swap, scratch = scratch[:lots[1]], scratch[lots[1]:]
     swapped, scratch = scratch[:lots[1]], scratch[lots[1]:]
     part, scratch = scratch[:lots[1]], scratch[lots[1]:]
-    landed, scratch = scratch[:lots[1]], scratch[lots[1]:]
-    x_sem, small_sem, send1, recv1, swap_send, swap_recv, send2, recv2 = scratch
+    x_sem, small_sem, own_sem, evid_sem, send1, recv1, swap_send, swap_recv, send2, recv2 = scratch
     me = lax.axis_index("blk")
     chips = n // 2
     chip, core = me // 2, lax.rem(me, 2)
@@ -51,10 +64,6 @@
     pl.semaphore_signal(barrier, inc=1, device_id=other, device_id_type=MESH)
     for d in range(1, chips):
         pl.semaphore_signal(barrier, inc=1, device_id=ahead(d), device_id_type=MESH)
-
-    def spot(c, b, k):
-        at = (c * TURNS + b) * owned + k
-        return at // DEPTH, at % DEPTH
 
     loads[0].wait()
     own = refs_ref[...].astype(jnp.float32)
@@ -64,14 +73,8 @@
         for b in range(TURNS):
             at = (c * TURNS + b) * LANES
             for k in range(owned):
-                j, row = spot(c, b, k)
+                j, row = spot(owned, c, b, k)
                 work[j, row:row + 1, :] = own[k:k + 1, at:at + LANES]
-
-    def each(parts):
-        first = 0
-        for lot, count in enumerate(parts):
-            yield lot, first, count
-            first += count
 
     for lot, first, count in each(parts_in):
         for j in range(count):
@@ -120,7 +123,7 @@
     lots_left = list(each(parts_in))
     ready = 0
     for c in range(CYCLES):
-        while ready <= spot(c, TURNS - 1, owned - 1)[0]:
+        while ready <= spot(owned, c, TURNS - 1, owned - 1)[0]:
             lot, first, count = lots_left.pop(0)
             spread(lot, first, count)
             ready = first + count
@@ -128,7 +131,7 @@
         for b in range(TURNS):
             column = []
             for k in range(owned):
-                j, row = spot(c, b, k)
+                j, row = spot(owned, c, b, k)
                 column.append(work[j, pl.ds(row, n, stride=DEPTH), :])
             pieces.append(jnp.concatenate(column, axis=0))
         ref_c = jnp.concatenate(pieces, axis=1)
@@ -151,6 +154,8 @@
     scaled = jnp.exp(logits - top)
     total = jnp.sum(scaled, axis=0, keepdims=True)
     evid_ref[...] = top + jnp.log(total)
+    evid_copy = pltpu.make_async_copy(evid_ref, evid_hbm, evid_sem)
+    evid_copy.start()
 
     slot = lax.broadcasted_iota(jnp.int32, (n, rows), 0)
     side = (slot >= chips).astype(jnp.int32)
@@ -172,7 +177,7 @@
 
     def put(c, b, value):
         for k in range(owned):
-            j, row = spot(c, b, k)
+            j, row = spot(owned, c, b, k)
             work[j, pl.ds(row, n, stride=DEPTH), :] = value[k * n:(k + 1) * n]
 
     mass = jnp.broadcast_to(mass, (classes, LANES))
@@ -180,7 +185,7 @@
     lane = lax.broadcasted_iota(jnp.int32, (classes, LANES), 1)
     put(CYCLES, 0, jnp.where(lane < LANES // 2, mass_high, mass - mass_high))
 
-    swaps, scatters = [], []
+    swaps, scatters, own_copies = [], [], []
 
     def give(lot, first, count):
         for d in range(chips):
@@ -208,7 +213,11 @@
                     src_ref=part[lot].at[d], dst_ref=landed[lot].at[d], send_sem=send2.at[lot, d],
                     recv_sem=recv2.at[lot, d], device_id=behind(d), device_id_type=MESH)
                 copy.start()
-                scatters.append((lot, d, first, count, copy))
+                scatters.append(copy)
+        copy = pltpu.make_async_copy(
+            work.at[first:first + count, 0:DEPTH], own_hbm.at[first:first + count], own_sem.at[lot])
+        copy.start()
+        own_copies.append(copy)
 
     lots_left = list(each(parts_out))
     given = []
@@ -236,27 +245,44 @@
             copy.wait_send()
     for copy in swaps:
         copy.wait_send()
+    for copy in own_copies:
+        copy.wait()
+    evid_copy.wait()
+    for copy in scatters:
+        copy.wait()
+
+
+def finish(owned, parts_out, *refs):
+    lots = len(parts_out)
+    landed, (own_hbm, evid_hbm, sums_ref, mass_ref, evid_ref) = refs[:lots], refs[lots:lots + 5]
+    arrived, (work, evid, sems) = refs[lots + 5:-3], refs[-3:]
+    loads = [pltpu.make_async_copy(src, dst, sems.at[i]) for i, (src, dst) in enumerate(
+        zip((own_hbm, evid_hbm, *landed), (work, evid, *arrived)))]
+    for load in loads:
+        load.start()
+    loads[0].wait()
     for lot, first, count in each(parts_out):
-        mine = [one for one in scatters if one[0] == lot]
-        acc = [work[first + j, 0:DEPTH, :] for j in range(count)]
-        for _, d, _, _, copy in mine:
-            copy.wait_recv()
-            for j in range(count):
-                acc[j] = acc[j] + landed[lot][d, :, j * LANES:(j + 1) * LANES].astype(jnp.float32)
+        loads[2 + lot].wait()
         for j in range(count):
-            work[first + j, 0:DEPTH, :] = acc[j]
+            acc = work[first + j]
+            for d in range(1, arrived[lot].shape[0]):
+                acc = acc + arrived[lot][d, :, j * LANES:(j + 1) * LANES].astype(jnp.float32)
+            work[first + j] = acc
     for c in range(CYCLES):
         for b in range(TURNS):
             at = (c * TURNS + b) * LANES
             for k in range(owned):
-                j, row = spot(c, b, k)
+                j, row = spot(owned, c, b, k)
                 sums_ref[k:k + 1, at:at + LANES] = work[j, row:row + 1, :]
+    lane = lax.broadcasted_iota(jnp.int32, (1, LANES), 1)
+    mass = jnp.zeros((1, LANES), jnp.float32)
     for k in range(owned):
-        j, row = spot(CYCLES, 0, k)
+        j, row = spot(owned, CYCLES, 0, k)
         tail = work[j, row:row + 1, :]
-        mass_ref[k:k + 1, :] = tail + pltpu.roll(tail, LANES // 2, 1)
-    for *_, copy in scatters:
-        copy.wait_send()
+        mass = jnp.where(lane == k, tail + pltpu.roll(tail, LANES // 2, 1), mass)
+    mass_ref[...] = mass[:, 0:owned]
+    loads[1].wait()
+    evid_ref[...] = evid[...]
 
 
 def local(particles, references, inv_noise, assign):
@@ -266,49 +292,68 @@
     chips = n // 2
     columns = -(-(CYCLES * TURNS + 1) * owned // DEPTH)
     parts_in = (columns - columns * 2 // 5, columns * 2 // 5)
-    parts_out = parts_in[::-1]
+    parts_out = (columns * 2 // 5, columns - columns * 2 // 5 - columns // 5, columns // 5)
     vmem = pl.BlockSpec(memory_space=pltpu.VMEM)
     hbm = pl.BlockSpec(memory_space=pltpu.HBM)
 
     def slots(count, parts):
         return [pltpu.VMEM((count, DEPTH, part * LANES), jnp.bfloat16) for part in parts]
 
-    sums, mass, evid = pl.pallas_call(
+    shares = pl.pallas_call(
         functools.partial(kernel, n, owned, parts_in, parts_out),
         out_shape=(
-            jax.ShapeDtypeStruct((owned, width), jnp.float32),
-            jax.ShapeDtypeStruct((owned, LANES), jnp.float32),
+            *(jax.ShapeDtypeStruct((chips, DEPTH, part * LANES), jnp.bfloat16) for part in parts_out),
+            jax.ShapeDtypeStruct((columns, DEPTH, LANES), jnp.float32),
             jax.ShapeDtypeStruct((1, rows), jnp.float32),
         ),
         in_specs=[hbm] * 4,
-        out_specs=(vmem, vmem, vmem),
+        out_specs=(hbm,) * (len(parts_out) + 2),
         scratch_shapes=[
             pltpu.VMEM((rows, width), jnp.bfloat16),
             pltpu.VMEM((width, rows), jnp.bfloat16),
             pltpu.VMEM((owned, width), jnp.bfloat16),
             pltpu.VMEM((1, rows), jnp.float32),
             pltpu.VMEM((TOPK, rows), jnp.int32),
+            pltpu.VMEM((1, rows), jnp.float32),
             pltpu.VMEM((columns, n * DEPTH, LANES), jnp.float32),
             *slots(n, parts_in),
             *slots(chips, parts_out),
             *slots(chips, parts_out),
             *slots(chips, parts_out),
-            *slots(chips, parts_out),
             pltpu.SemaphoreType.DMA,
             pltpu.SemaphoreType.DMA((3,)),
-            pltpu.SemaphoreType.DMA((2, n)),
-            pltpu.SemaphoreType.DMA((2, n)),
-            pltpu.SemaphoreType.DMA((2,)),
-            pltpu.SemaphoreType.DMA((2,)),
-            pltpu.SemaphoreType.DMA((2, chips)),
-            pltpu.SemaphoreType.DMA((2, chips)),
+            pltpu.SemaphoreType.DMA((len(parts_out),)),
+            pltpu.SemaphoreType.DMA,
+            pltpu.SemaphoreType.DMA((len(parts_in), n)),
+            pltpu.SemaphoreType.DMA((len(parts_in), n)),
+            pltpu.SemaphoreType.DMA((len(parts_out),)),
+            pltpu.SemaphoreType.DMA((len(parts_out),)),
+            pltpu.SemaphoreType.DMA((len(parts_out), chips)),
+            pltpu.SemaphoreType.DMA((len(parts_out), chips)),
         ],
         compiler_params=pltpu.CompilerParams(
             collective_id=0, has_side_effects=True, vmem_limit_bytes=64 * 1024 * 1024 - 65536),
         cost_estimate=pl.CostEstimate(
             flops=6 * rows * n * owned * ROT * width, bytes_accessed=2 * rows * width, transcendentals=rows * n * owned * ROT),
     )(particles, references, inv_noise.reshape(1, rows), assign.T)
-    return sums, mass[:, 0], evid.reshape(rows)
+    sums, mass, evid = pl.pallas_call(
+        functools.partial(finish, owned, parts_out),
+        out_shape=(
+            jax.ShapeDtypeStruct((owned, width), jnp.float32),
+            jax.ShapeDtypeStruct((1, owned), jnp.float32),
+            jax.ShapeDtypeStruct((1, rows), jnp.float32),
+        ),
+        in_specs=[hbm] * (len(parts_out) + 2),
+        out_specs=(vmem, vmem, vmem),
+        scratch_shapes=[
+            *slots(chips, parts_out),
+            pltpu.VMEM((columns, DEPTH, LANES), jnp.float32),
+            pltpu.VMEM((1, rows), jnp.float32),
+            pltpu.SemaphoreType.DMA((len(parts_out) + 2,)),
+        ],
+        compiler_params=pltpu.CompilerParams(vmem_limit_bytes=64 * 1024 * 1024 - 65536),
+    )(*shares)
+    return sums, mass.reshape(owned), evid.reshape(rows)
 
 
 def solution(mesh):

time: 30.7 us -> 27.9 us (0.909)
  local copies, waits for them, and re-layouts: 3.82 us -> 0 us
  Pallas kernels: 26 us -> 27.1 us
    unnamed x2 -> x0, local copies, waits for them, and re-layouts: 2.53 us -> none
    pallas_call x0 -> x1, Pallas kernels: none -> 1.67 us  [local(): pl.pallas_call(functools.partial(finish, owned, parts_out), out_shape=(ja...]
    slice x1 -> x0, local copies, waits for them, and re-layouts: 1.29 us -> none  [local(): return (sums, mass[:, 0], evid.reshape(rows))]
    pallas_call x1, Pallas kernels: 26 us -> 25.4 us  [local(): pl.pallas_call(functools.partial(kernel, n, owned, parts_in, parts_out),...]
where the time goes in v4:
time: 27.9 us; the launch traced here: 27.7 us
  Pallas kernels  27.1 us (97%)
  between operations  0.64 us (2%)
    pallas_call x1, Pallas kernels, local(): pl.pallas_call(functools.partial(kernel, n, owned, parts_in, parts_out),...  25.4 us
    pallas_call x1, Pallas kernels, local(): pl.pallas_call(functools.partial(finish, owned, parts_out), out_shape=(ja...  1.67 us

profile of v4, /device:TPU:0, one launch (start us, length us, event | category | flops | bytes accessed | tf_op | source)
XLA Modules:
  0.0 27.7 jit_solution(4187445698937401664)
XLA Ops:
  0.6 25.4 %shard_map.67 = (bf16[8,16,256]{2,1,0:T(8,128)(2,1)}, bf16[8,16,256]{2,1,0:T(8,128)(2,1)}, bf16[8,16,128]{2,1,0:T(8,128)(2,1)}, f32[5,16,128]{2,1,0:T(8,128)}, f32[1,128]{1,0:T(1,128)}) custom-call(bf16[128,4608]{1,0:T(8,128)(2,1)} %x_hbm.1, bf16[2,4608]{1,0:T(2,128)(2,1)} %refs_hbm.1, f32[1,128]{1,0:T(1,128)} %bitcast.5, s32[2,128]{1,0:T(2,128)} %bitcast.4), custom_call_target="tpu_custom_call" | custom-call | flops 1358954496 | bytes 1179648 | tf_op jit(solution)/shard_map/pallas_call | solution.py:302
  26.1 1.7 %shard_map.68 = (f32[2,4608]{1,0:T(2,128)}, f32[1,2]{1,0:T(1,128)}, f32[1,128]{1,0:T(1,128)}) custom-call(bf16[8,16,256]{2,1,0:T(8,128)(2,1)} %get-tuple-element.11.refs_0_, bf16[8,16,256]{2,1,0:T(8,128)(2,1)} %get-tuple-element.12.refs_1_, bf16[8,16,128]{2,1,0:T(8,128)(2,1)} %get-tuple-element.13.refs_2_, f32[5,16,128]{2,1,0:T(8,128)} %get-tuple-element.14.refs_3_, ...), custom_call_target="tpu_custom_call" | custom-call | tf_op jit(solution)/shard_map/pallas_call | solution.py:339

commit v5 on v4

--- a/solution.py
+++ b/solution.py
@@ -37,7 +37,6 @@
     own_hbm, evid_hbm, x_ref, xt_ref, refs_ref, inv_ref, assign_ref, evid_ref, work = scratch[:9]
     scratch = scratch[9:]
     held, scratch = scratch[:lots[0]], scratch[lots[0]:]
-    swap, scratch = scratch[:lots[1]], scratch[lots[1]:]
     swapped, scratch = scratch[:lots[1]], scratch[lots[1]:]
     part, scratch = scratch[:lots[1]], scratch[lots[1]:]
     x_sem, small_sem, own_sem, evid_sem, send1, recv1, swap_send, swap_recv, send2, recv2 = scratch
@@ -96,8 +95,13 @@
         gathers.append(copies)
     for load in loads[1:]:
         load.wait()
-    for at in range(0, x_ref.shape[1], LANES):
-        xt_ref[at:at + LANES, :] = x_ref[:, at:at + LANES].T
+
+    def turn_over(start, stop):
+        for at in range(start * LANES, min(stop * LANES, x_ref.shape[1]), LANES):
+            xt_ref[at:at + LANES, :] = x_ref[:, at:at + LANES].T
+
+    tiles = x_ref.shape[1] // LANES
+    step = -(-tiles // (chips - 1))
 
     def shifted(c):
         blocks = [x_ref[:, (c * TURNS + b) * LANES:(c * TURNS + b + 1) * LANES] for b in range(TURNS)]
@@ -105,11 +109,16 @@
             [jnp.concatenate([blocks[(b + q) % TURNS] for b in range(TURNS)], axis=1)
              for q in range(TURNS)], axis=0)
 
+    def forward(lot):
+        copies = gathers[lot]
+        for d in range(1, chips):
+            if lot == 0:
+                turn_over((d - 1) * step, d * step)
+            copies[d].wait_recv()
+            copies[chips + d] = move(lot, d, chips + d, other)
+
     def spread(lot, first, count):
         copies = gathers[lot]
-        for d in range(1, chips):
-            copies[d].wait_recv()
-            copies[chips + d] = move(lot, d, chips + d, other)
         for d in range(chips):
             copies[chips + d].wait_recv()
         for d in range(n):
@@ -122,7 +131,11 @@
     turned = []
     lots_left = list(each(parts_in))
     ready = 0
+    forward(0)
     for c in range(CYCLES):
+        if c == 2:
+            for lot in range(1, lots[0]):
+                forward(lot)
         while ready <= spot(owned, c, TURNS - 1, owned - 1)[0]:
             lot, first, count = lots_left.pop(0)
             spread(lot, first, count)
@@ -172,8 +185,6 @@
     turn = SHIFTS * classes
     weight = jnp.concatenate([weight[q * turn:(q + 1) * turn] for q in range(TURNS)], axis=1)
     high = weight.astype(jnp.bfloat16)
-    low = (weight - high.astype(jnp.float32)).astype(jnp.bfloat16)
-    both = jnp.concatenate([high, low], axis=0)
 
     def put(c, b, value):
         for k in range(owned):
@@ -188,13 +199,9 @@
     swaps, scatters, own_copies = [], [], []
 
     def give(lot, first, count):
-        for d in range(chips):
-            for j in range(count):
-                swap[lot][d, :, j * LANES:(j + 1) * LANES] = (
-                    work[first + j, (chips + d) * DEPTH:(chips + d + 1) * DEPTH, :].astype(jnp.bfloat16))
         copy = pltpu.make_async_remote_copy(
-            src_ref=swap[lot], dst_ref=swapped[lot], send_sem=swap_send.at[lot], recv_sem=swap_recv.at[lot],
-            device_id=other, device_id_type=MESH)
+            src_ref=work.at[first:first + count, chips * DEPTH:n * DEPTH], dst_ref=swapped[lot],
+            send_sem=swap_send.at[lot], recv_sem=swap_recv.at[lot], device_id=other, device_id_type=MESH)
         copy.start()
         swaps.append(copy)
 
@@ -203,7 +210,7 @@
         for d in (*range(1, chips), 0):
             for j in range(count):
                 both_cores = (work[first + j, d * DEPTH:(d + 1) * DEPTH, :]
-                              + swapped[lot][d, :, j * LANES:(j + 1) * LANES].astype(jnp.float32))
+                              + swapped[lot][j, d * DEPTH:(d + 1) * DEPTH, :])
                 if d:
                     part[lot][d, :, j * LANES:(j + 1) * LANES] = both_cores.astype(jnp.bfloat16)
                 else:
@@ -222,10 +229,13 @@
     lots_left = list(each(parts_out))
     given = []
     for c in range(CYCLES):
-        mixed = jnp.dot(both, shifted(c), preferred_element_type=jnp.float32)
+        if c % 2 == 0:
+            mixed = jnp.dot(
+                high, jnp.concatenate([shifted(c), shifted(c + 1)], axis=1), preferred_element_type=jnp.float32)
+        at = c % 2 * ANGLES
         out = None
         for s in range(SHIFTS):
-            piece = mixed[s * classes:(s + 1) * classes] + mixed[(SHIFTS + s) * classes:(SHIFTS + s + 1) * classes]
+            piece = mixed[s * classes:(s + 1) * classes, at:at + ANGLES]
             if s:
                 piece = pltpu.roll(piece, ANGLES - s * STEP, 1)
             out = piece if out is None else out + piece
@@ -317,8 +327,7 @@
             pltpu.VMEM((1, rows), jnp.float32),
             pltpu.VMEM((columns, n * DEPTH, LANES), jnp.float32),
             *slots(n, parts_in),
-            *slots(chips, parts_out),
-            *slots(chips, parts_out),
+            *(pltpu.VMEM((part, chips * DEPTH, LANES), jnp.float32) for part in parts_out),
             *slots(chips, parts_out),
             pltpu.SemaphoreType.DMA,
             pltpu.SemaphoreType.DMA((3,)),

time: 27.9 us -> 26.3 us (0.943)
  Pallas kernels: 27.1 us -> 25.5 us
    pallas_call x1, Pallas kernels: 25.4 us -> 23.8 us  [local(): pl.pallas_call(functools.partial(kernel, n, owned, parts_in, parts_out),...]
where the time goes in v5:
time: 26.3 us; the launch traced here: 26.1 us
  Pallas kernels  25.5 us (97%)
  between operations  0.64 us (2%)
    pallas_call x1, Pallas kernels, local(): pl.pallas_call(functools.partial(kernel, n, owned, parts_in, parts_out),...  23.8 us
    pallas_call x1, Pallas kernels, local(): pl.pallas_call(functools.partial(finish, owned, parts_out), out_shape=(ja...  1.67 us

profile of v5, /device:TPU:0, one launch (start us, length us, event | category | flops | bytes accessed | tf_op | source)
XLA Modules:
  0.0 26.1 jit_solution(13806706639853573317)
XLA Ops:
  0.6 23.8 %shard_map.67 = (bf16[8,16,256]{2,1,0:T(8,128)(2,1)}, bf16[8,16,256]{2,1,0:T(8,128)(2,1)}, bf16[8,16,128]{2,1,0:T(8,128)(2,1)}, f32[5,16,128]{2,1,0:T(8,128)}, f32[1,128]{1,0:T(1,128)}) custom-call(bf16[128,4608]{1,0:T(8,128)(2,1)} %x_hbm.1, bf16[2,4608]{1,0:T(2,128)(2,1)} %refs_hbm.1, f32[1,128]{1,0:T(1,128)} %bitcast.5, s32[2,128]{1,0:T(2,128)} %bitcast.4), custom_call_target="tpu_custom_call" | custom-call | flops 1358954496 | bytes 1179648 | tf_op jit(solution)/shard_map/pallas_call | solution.py:312
  24.5 1.7 %shard_map.68 = (f32[2,4608]{1,0:T(2,128)}, f32[1,2]{1,0:T(1,128)}, f32[1,128]{1,0:T(1,128)}) custom-call(bf16[8,16,256]{2,1,0:T(8,128)(2,1)} %get-tuple-element.11.refs_0_, bf16[8,16,256]{2,1,0:T(8,128)(2,1)} %get-tuple-element.12.refs_1_, bf16[8,16,128]{2,1,0:T(8,128)(2,1)} %get-tuple-element.13.refs_2_, f32[5,16,128]{2,1,0:T(8,128)} %get-tuple-element.14.refs_3_, ...), custom_call_target="tpu_custom_call" | custom-call | tf_op jit(solution)/shard_map/pallas_call | solution.py:348

commit v6 on v5

--- a/solution.py
+++ b/solution.py
@@ -302,7 +302,7 @@
     chips = n // 2
     columns = -(-(CYCLES * TURNS + 1) * owned // DEPTH)
     parts_in = (columns - columns * 2 // 5, columns * 2 // 5)
-    parts_out = (columns * 2 // 5, columns - columns * 2 // 5 - columns // 5, columns // 5)
+    parts_out = (columns * 2 // 5, columns // 5, columns - columns * 2 // 5 - columns // 5)
     vmem = pl.BlockSpec(memory_space=pltpu.VMEM)
     hbm = pl.BlockSpec(memory_space=pltpu.HBM)
 

time: 26.3 us -> 25.9 us (0.985)
  Pallas kernels: 25.5 us -> 25.1 us
    pallas_call x1, Pallas kernels: 23.8 us -> 23.4 us  [local(): pl.pallas_call(functools.partial(kernel, n, owned, parts_in, parts_out),...]
where the time goes in v6:
time: 25.9 us; the launch traced here: 25.7 us
  Pallas kernels  25.1 us (97%)
  between operations  0.64 us (2%)
    pallas_call x1, Pallas kernels, local(): pl.pallas_call(functools.partial(kernel, n, owned, parts_in, parts_out),...  23.4 us
    pallas_call x1, Pallas kernels, local(): pl.pallas_call(functools.partial(finish, owned, parts_out), out_shape=(ja...  1.68 us

profile of v6, /device:TPU:0, one launch (start us, length us, event | category | flops | bytes accessed | tf_op | source)
XLA Modules:
  0.0 25.7 jit_solution(6999418635239181397)
XLA Ops:
  0.6 23.4 %shard_map.67 = (bf16[8,16,256]{2,1,0:T(8,128)(2,1)}, bf16[8,16,128]{2,1,0:T(8,128)(2,1)}, bf16[8,16,256]{2,1,0:T(8,128)(2,1)}, f32[5,16,128]{2,1,0:T(8,128)}, f32[1,128]{1,0:T(1,128)}) custom-call(bf16[128,4608]{1,0:T(8,128)(2,1)} %x_hbm.1, bf16[2,4608]{1,0:T(2,128)(2,1)} %refs_hbm.1, f32[1,128]{1,0:T(1,128)} %bitcast.5, s32[2,128]{1,0:T(2,128)} %bitcast.4), custom_call_target="tpu_custom_call" | custom-call | flops 1358954496 | bytes 1179648 | tf_op jit(solution)/shard_map/pallas_call | solution.py:312
  24.0 1.7 %shard_map.68 = (f32[2,4608]{1,0:T(2,128)}, f32[1,2]{1,0:T(1,128)}, f32[1,128]{1,0:T(1,128)}) custom-call(bf16[8,16,256]{2,1,0:T(8,128)(2,1)} %get-tuple-element.11.refs_0_, bf16[8,16,128]{2,1,0:T(8,128)(2,1)} %get-tuple-element.12.refs_1_, bf16[8,16,256]{2,1,0:T(8,128)(2,1)} %get-tuple-element.13.refs_2_, f32[5,16,128]{2,1,0:T(8,128)} %get-tuple-element.14.refs_3_, ...), custom_call_target="tpu_custom_call" | custom-call | tf_op jit(solution)/shard_map/pallas_call | solution.py:348

commit v7 on v6

--- a/solution.py
+++ b/solution.py
@@ -302,7 +302,7 @@
     chips = n // 2
     columns = -(-(CYCLES * TURNS + 1) * owned // DEPTH)
     parts_in = (columns - columns * 2 // 5, columns * 2 // 5)
-    parts_out = (columns * 2 // 5, columns // 5, columns - columns * 2 // 5 - columns // 5)
+    parts_out = (columns // 5,) * 3 + (columns - columns // 5 * 3,)
     vmem = pl.BlockSpec(memory_space=pltpu.VMEM)
     hbm = pl.BlockSpec(memory_space=pltpu.HBM)
 

time: 25.9 us -> 26.8 us (1.035)
  Pallas kernels: 25.1 us -> 26 us
    pallas_call x1, Pallas kernels: 23.4 us -> 24.3 us  [local(): pl.pallas_call(functools.partial(kernel, n, owned, parts_in, parts_out),...]
where the time goes in v7:
time: 26.8 us; the launch traced here: 26.6 us
  Pallas kernels  26 us (97%)
  between operations  0.64 us (2%)
    pallas_call x1, Pallas kernels, local(): pl.pallas_call(functools.partial(kernel, n, owned, parts_in, parts_out),...  24.3 us
    pallas_call x1, Pallas kernels, local(): pl.pallas_call(functools.partial(finish, owned, parts_out), out_shape=(ja...  1.69 us

profile of v7, /device:TPU:0, one launch (start us, length us, event | category | flops | bytes accessed | tf_op | source)
XLA Modules:
  0.0 26.6 jit_solution(18311112987137427933)
XLA Ops:
  0.6 24.3 %shard_map.67 = (bf16[8,16,128]{2,1,0:T(8,128)(2,1)}, bf16[8,16,128]{2,1,0:T(8,128)(2,1)}, bf16[8,16,128]{2,1,0:T(8,128)(2,1)}, bf16[8,16,256]{2,1,0:T(8,128)(2,...) custom-call(bf16[128,4608]{1,0:T(8,128)(2,1)} %x_hbm.1, bf16[2,4608]{1,0:T(2,128)(2,1)} %refs_hbm.1, f32[1,128]{1,0:T(1,128)} %bitcast.5, ...), custom_call_target="tpu_custom_call" | custom-call | flops 1358954496 | bytes 1179648 | tf_op jit(solution)/shard_map/pallas_call | solution.py:312
  24.9 1.7 %shard_map.68 = (f32[2,4608]{1,0:T(2,128)}, f32[1,2]{1,0:T(1,128)}, f32[1,128]{1,0:T(1,128)}) custom-call(bf16[8,16,128]{2,1,0:T(8,128)(2,1)} %get-tuple-element.12.refs_0_, bf16[8,16,128]{2,1,0:T(8,128)(2,1)} %get-tuple-element.13.refs_1_, bf16[8,16,128]{2,1,0:T(8,128)(2,1)} %get-tuple-element.14.refs_2_, bf16[8,16,256]{2,1,0:T(8,128)(2,1)} %get-tuple-element.15.refs_3_, ...), custom_call_target="tpu_custom_call" | custom-call | tf_op jit(solution)/shard_map/pallas_call | solution.py:348
